TPU v7x, 256 devices: a whole 4x4x8 slice. The times are simulated.
256 devices in a mesh: row: 16 (over x, y), col: 16 (over z, core).
Axes of the slice: x: 4, y: 4, z: 8, core: 2. Of those that a mesh axis runs over, the one named last changes fastest.
Arguments:
- matrix_cyclic: float32 [16384, 16384], P('row', 'col'), as said below
Outputs:
- reduced: float32 [16384, 16384], P('row', 'col')
- band_factors: float32 [2, 256, 256], replicated
Inputs may be any that keep to these rules, and one draw needn't show every extreme that they name: `matrix_cyclic`: in global order the matrix is symmetric up to rounding.
All inputs are finite; a program needn't handle non-finite values.
Results may differ from a plain program's by a relative error of at most 0.00016.
Values sent between devices are 32-bit elements; how exact they have to be, the bound alone decides.
A program may use at most 128 MiB of HBM per device.

v0:
```python
import math

import jax
import jax.numpy as jnp
from jax import lax
from jax.sharding import PartitionSpec as P

PANEL = 256


def from_root(array, axis, root):
    mine = lax.axis_index(axis) == root
    return lax.psum(jnp.where(mine, array, jnp.zeros_like(array)), axis)


def matmul(left, right):
    return jnp.dot(left, right, precision=lax.Precision.HIGHEST, preferred_element_type=jnp.float32)


def invert_near_identity(operand):
    identity = jnp.eye(operand.shape[0], dtype=jnp.float32)
    estimate = identity
    for iteration in range(6):
        estimate = matmul(estimate, 2.0 * identity - matmul(operand, estimate))
    return estimate


def shards(matrix_cyclic):
    rows_grid = lax.axis_size("row")
    cols_grid = lax.axis_size("col")
    row_index = lax.axis_index("row")
    col_index = lax.axis_index("col")
    local_rows, local_cols = matrix_cyclic.shape
    width = PANEL
    row_blocks = local_rows // width
    col_blocks = local_cols // width
    order = col_blocks * width * cols_grid
    group_stride = cols_grid // rows_grid
    row_global = jnp.arange(row_blocks, dtype=jnp.int32) * rows_grid + row_index
    col_global = jnp.arange(col_blocks, dtype=jnp.int32) * cols_grid + col_index
    source_row = col_index % rows_grid
    column_offset = col_index // rows_grid
    identity = jnp.eye(width, dtype=jnp.float32)

    def pick_columns(received):
        shaped = received.reshape(col_blocks, group_stride, width, width)
        chosen = lax.dynamic_index_in_dim(shaped, column_offset, axis=1, keepdims=False)
        return chosen.reshape(local_cols, width)

    def prepare(panel_source, panel_index):
        panel = from_root(panel_source, "col", panel_index % cols_grid)
        live = (row_global > panel_index).astype(jnp.float32)
        top_flag = (row_global == panel_index + 1).astype(jnp.float32)
        blocks = panel.reshape(row_blocks, width, width) * live[:, None, None]
        panel = blocks.reshape(local_rows, width)
        top_block = jnp.sum(blocks * top_flag[:, None, None], axis=0)
        gram, top_block = lax.psum((matmul(panel.T, panel), top_block), "row")
        lower_factor = jnp.linalg.cholesky(gram)
        q_rows = jax.scipy.linalg.solve_triangular(lower_factor, panel.T, lower=True).T
        q_top = jax.scipy.linalg.solve_triangular(lower_factor, top_block.T, lower=True).T
        inverse_t = invert_near_identity(identity - q_top.T)
        unit_rows = (identity[None, :, :] * top_flag[:, None, None]).reshape(local_rows, width)
        w_rows = unit_rows - q_rows
        w_cols = pick_columns(from_root(w_rows, "row", source_row))
        return (w_rows, w_cols, inverse_t, lower_factor)

    def finish(matrix, prepared):
        w_rows, w_cols, inverse_t, lower_factor = prepared
        x_rows = lax.psum(matmul(matrix, w_cols), "col")
        middle = lax.psum(matmul(w_rows.T, x_rows), "row")
        sym_block = matmul(matmul(inverse_t.T, middle), inverse_t)
        u_rows = matmul(x_rows, inverse_t) - 0.5 * matmul(w_rows, sym_block)
        u_cols = pick_columns(from_root(u_rows, "row", source_row))
        left = jnp.concatenate([w_rows, u_rows], axis=1)
        right = jnp.concatenate([u_cols, w_cols], axis=1)
        return (left, right)

    matrix = matrix_cyclic
    first_start = 0 // cols_grid * width
    prepared = prepare(matrix[:, first_start : first_start + width], 0)
    upper_first = prepared[3].T
    left, right = finish(matrix, prepared)
    next_start = 1 // cols_grid * width
    matrix = matrix - matmul(left, right.T)
    prepared = prepare(matrix[:, next_start : next_start + width], 1)
    upper_second = prepared[3].T
    left, right = finish(matrix, prepared)
    matrix = matrix - matmul(left, right.T)
    row_keep = jnp.repeat((row_global >= 2).astype(jnp.float32), width)
    col_keep = jnp.repeat((col_global >= 2).astype(jnp.float32), width)
    reduced = matrix * row_keep[:, None] * col_keep[None, :]
    band_factors = jnp.stack([upper_first, upper_second]) / math.sqrt(order)
    return (reduced, band_factors)


def solution(mesh):
    return jax.shard_map(
        shards,
        mesh=mesh,
        in_specs=(P("row", "col"),),
        out_specs=(P("row", "col"), P()),
        check_vma=False,
    )
```

profile of v0, /device:TPU:1, one launch (start us, length us, event | category | flops | bytes accessed | tf_op | source)
XLA Modules:
  0.0 1451.5 jit_solution(18059665460420172853)
XLA Ops:
  7.2 5.3 copy.18
  12.6 2.4 slice_select_fusion.1
  15.7 114.5 %all-reduce.16.cloned.1.call-done = f32[1024,256]{0,1:T(8,128)} async-done(((f32[1024,256]{0,1:T(8,128)}), f32[1024,256]{0,1:T(8,128)}) %all-reduce.16.cloned.1.call-update) | async-done | bytes 1048592 | tf_op jit(solution)/shard_map/psum | solution.py:13
  130.3 3.3 fusion.18
  134.2 1.3 multiply_bitcast_fusion.1
  135.5 92.3 %all-reduce.18.cloned.1.call-done = f32[256,256]{0,1:T(8,128)} async-done(((f32[256,256]{0,1:T(8,128)}), f32[256,256]{0,1:T(8,128)}) %all-reduce.18.cloned.1.call-update) | async-done | bytes 262160 | tf_op jit(solution)/shard_map/psum | solution.py:57
  229.9 11.7 cholesky.130
  242.3 9.8 custom-call.17
  252.6 11.7 cholesky.147
  267.2 4.2 while.8
  268.0 1.4 bitcast_dynamic-update-slice_fusion.4
  270.0 1.4 bitcast_dynamic-update-slice_fusion.4
  271.3 19.7 %custom-call.18 = f32[2,128,128]{1,2,0:T(8,128)S(1)} custom-call(f32[2,128,128]{2,1,0:T(8,128)S(1)} %get-tuple-element.33), custom_call_target="InvertDiagBlocksLowerTriangular" | custom-call | tf_op jit(solution)/shard_map/jit(_solve_triangular)/triangular_solve | solution.py:59
  292.9 1.3 broadcast_select_fusion.3
  294.2 96.5 %all-reduce.20.cloned.1.call-done = f32[1024,256]{0,1:T(8,128)} async-done(((f32[1024,256]{0,1:T(8,128)}), f32[1024,256]{0,1:T(8,128)}) %all-reduce.20.cloned.1.call-update) | async-done | bytes 1048592 | tf_op jit(solution)/shard_map/psum | solution.py:13
  390.7 7.2 convolution_bitcast_fusion
  398.0 1.4 reshape.92
  399.4 2.7 multiply_reduce_fusion.1
  402.1 107.9 %all-reduce.22.cloned.1.call-done = f32[1024,256]{0,1:T(8,128)} async-done(((f32[1024,256]{0,1:T(8,128)}), f32[1024,256]{0,1:T(8,128)}) %all-reduce.22.cloned.1.call-update) | async-done | bytes 1048592 | tf_op jit(solution)/shard_map/psum | solution.py:69
  510.0 3.0 fusion.67
  513.2 94.6 %all-reduce.38.cloned.1.call-done = (f32[256,256]{1,0:T(8,128)}, f32[256,256]{1,0:T(8,128)}) async-done(((f32[256,256]{1,0:T(8,128)}, f32[256,256]{1,0:T(8,128)}), (f32[256,256]{1,0:T(8,128)}, f32[256,256]{1,0:T(8,128)})) %all-reduce.38.cloned.1.call-update) | async-done | bytes 524304 | tf_op jit(solution)/shard_map/psum | solution.py:57
  617.2 2.2 broadcast_select_fusion.2
  619.5 96.6 %all-reduce.24.cloned.1.call-done = f32[1024,256]{0,1:T(8,128)} async-done(((f32[1024,256]{0,1:T(8,128)}), f32[1024,256]{0,1:T(8,128)}) %all-reduce.24.cloned.1.call-update) | async-done | bytes 1048592 | tf_op jit(solution)/shard_map/psum | solution.py:13
  716.1 9.0 convolution_subtract_fusion
  725.1 2.0 copy-done
  728.5 111.9 %all-reduce.26.cloned.1.call-done = f32[1024,256]{0,1:T(8,128)} async-done(((f32[1024,256]{0,1:T(8,128)}), f32[1024,256]{0,1:T(8,128)}) %all-reduce.26.cloned.1.call-update) | async-done | bytes 1048592 | tf_op jit(solution)/shard_map/psum | solution.py:13
  840.4 3.3 fusion.16
  844.2 1.3 multiply_bitcast_fusion
  845.6 91.8 %all-reduce.28.cloned.1.call-done = f32[256,256]{0,1:T(8,128)} async-done(((f32[256,256]{0,1:T(8,128)}), f32[256,256]{0,1:T(8,128)}) %all-reduce.28.cloned.1.call-update) | async-done | bytes 262160 | tf_op jit(solution)/shard_map/psum | solution.py:57
  939.5 11.7 cholesky.164
  951.9 9.8 custom-call.20
  962.2 11.7 cholesky.181
  976.7 4.1 while.9
  977.5 1.4 bitcast_dynamic-update-slice_fusion.5
  979.5 1.4 bitcast_dynamic-update-slice_fusion.5
  980.8 19.7 %custom-call.21 = f32[2,128,128]{1,2,0:T(8,128)S(1)} custom-call(f32[2,128,128]{2,1,0:T(8,128)S(1)} %get-tuple-element.35), custom_call_target="InvertDiagBlocksLowerTriangular" | custom-call | tf_op jit(solution)/shard_map/jit(_solve_triangular)/triangular_solve | solution.py:59
  1003.7 96.5 %all-reduce.30.cloned.1.call-done = f32[1024,256]{0,1:T(8,128)} async-done(((f32[1024,256]{0,1:T(8,128)}), f32[1024,256]{0,1:T(8,128)}) %all-reduce.30.cloned.1.call-update) | async-done | bytes 1048592 | tf_op jit(solution)/shard_map/psum | solution.py:13
  1100.2 10.1 fusion.70
  1111.1 1.4 multiply_reduce_fusion
  1112.6 109.9 %all-reduce.32.cloned.1.call-done = f32[1024,256]{1,0:T(8,128)} async-done(((f32[1024,256]{1,0:T(8,128)}), f32[1024,256]{1,0:T(8,128)}) %all-reduce.32.cloned.1.call-update) | async-done | bytes 1048592 | tf_op jit(solution)/shard_map/psum | solution.py:69
  1222.4 2.9 fusion.77
  1225.5 95.0 %all-reduce.36.cloned.1.call-done = (f32[256,256]{1,0:T(8,128)}, f32[256,256]{1,0:T(8,128)}) async-done(((f32[256,256]{1,0:T(8,128)}, f32[256,256]{1,0:T(8,128)}), (f32[256,256]{1,0:T(8,128)}, f32[256,256]{1,0:T(8,128)})) %all-reduce.36.cloned.1.call-update) | async-done | bytes 524304 | tf_op jit(solution)/shard_map/psum | solution.py:57
  1329.9 2.1 broadcast_select_fusion
  1332.2 1.8 maximum_multiply_fusion
  1334.0 2.0 copy.24
  1336.0 92.6 %all-reduce.34.cloned.1.call-done = f32[1024,256]{0,1:T(8,128)} async-done(((f32[1024,256]{0,1:T(8,128)}), f32[1024,256]{0,1:T(8,128)}) %all-reduce.34.cloned.1.call-update) | async-done | bytes 1048592 | tf_op jit(solution)/shard_map/psum | solution.py:13
  1428.6 10.5 multiply_multiply_fusion
  1439.1 5.3 copy.23
  (140 shorter events, 40.1 us)
Async XLA Ops:
  7.2 123.1 %all-reduce.16.cloned.1.call-start = ((), (), s32[]{:S(2)}) async-start(), calls=%async_computation | async-start | bytes 2097152 | tf_op jit(solution)/shard_map/psum | solution.py:13
  14.9 212.9 %all-reduce.18.cloned.1.call-start = ((), (), s32[]{:S(2)}) async-start(), calls=%async_computation.1 | async-start | bytes 524288 | tf_op jit(solution)/shard_map/psum | solution.py:57
  133.6 257.1 %all-reduce.20.cloned.1.call-start = ((), (), s32[]{:S(2)}) async-start(), calls=%async_computation.2 | async-start | bytes 2097152 | tf_op jit(solution)/shard_map/psum | solution.py:13
  294.2 103.8 %copy-start.1 = (f32[1024,256]{0,1:T(8,128)S(1)}, f32[1024,256]{0,1:T(8,128)}, u32[]{:S(2)}) copy-start(f32[1024,256]{0,1:T(8,128)} %all-reduce.16.cloned.1.call-done) | copy-start | bytes 3145732
  294.2 215.8 %all-reduce.22.cloned.1.call-start = ((), (), s32[]{:S(2)}) async-start(), calls=%async_computation.3 | async-start | bytes 2097152 | tf_op jit(solution)/shard_map/psum | solution.py:69
  397.9 209.9 %all-reduce.38.cloned.1.call-start = ((), (), s32[]{:S(2)}) async-start(), calls=%async_computation.11 | async-start | bytes 1048576 | tf_op jit(solution)/shard_map/psum | solution.py:57
  513.0 203.1 %all-reduce.24.cloned.1.call-start = ((), (), s32[]{:S(2)}) async-start(), calls=%async_computation.4 | async-start | bytes 2097152 | tf_op jit(solution)/shard_map/psum | solution.py:13
  610.8 4.3 copy-start.7
  611.5 4.6 copy-start.3
  619.4 221.0 %all-reduce.26.cloned.1.call-start = ((), (), s32[]{:S(2)}) async-start(), calls=%async_computation.5 | async-start | bytes 2097152 | tf_op jit(solution)/shard_map/psum | solution.py:13
  725.1 2.0 copy-start
  728.3 209.1 %all-reduce.28.cloned.1.call-start = ((), (), s32[]{:S(2)}) async-start(), calls=%async_computation.6 | async-start | bytes 524288 | tf_op jit(solution)/shard_map/psum | solution.py:57
  843.8 256.4 %all-reduce.30.cloned.1.call-start = ((), (), s32[]{:S(2)}) async-start(), calls=%async_computation.7 | async-start | bytes 2097152 | tf_op jit(solution)/shard_map/psum | solution.py:13
  1003.7 106.9 %copy-start.2 = (f32[1024,256]{0,1:T(8,128)S(1)}, f32[1024,256]{0,1:T(8,128)}, u32[]{:S(2)}) copy-start(f32[1024,256]{0,1:T(8,128)} %all-reduce.26.cloned.1.call-done) | copy-start | bytes 3145732
  1003.7 218.8 %all-reduce.32.cloned.1.call-start = ((), (), s32[]{:S(2)}) async-start(), calls=%async_computation.8 | async-start | bytes 2097152 | tf_op jit(solution)/shard_map/psum | solution.py:69
  1110.3 210.1 %all-reduce.36.cloned.1.call-start = ((), (), s32[]{:S(2)}) async-start(), calls=%async_computation.10 | async-start | bytes 1048576 | tf_op jit(solution)/shard_map/psum | solution.py:57
  1225.4 203.2 %all-reduce.34.cloned.1.call-start = ((), (), s32[]{:S(2)}) async-start(), calls=%async_computation.9 | async-start | bytes 2097152 | tf_op jit(solution)/shard_map/psum | solution.py:13
  1323.4 4.3 copy-start.8
  1324.1 4.6 copy-start.4
  1328.3 3.9 copy-start.6
  1329.9 98.7 %copy-start.5 = (f32[1024,256]{0,1:T(8,128)S(1)}, f32[1024,256]{0,1:T(8,128)}, u32[]{:S(2)}) copy-start(f32[1024,256]{0,1:T(8,128)} %all-reduce.30.cloned.1.call-done) | copy-start | bytes 3145732
Sparse Core Ops, SparseCore 0:
  15.1 115.1 all-reduce.15
  134.3 93.4 all-reduce.17
  294.3 96.3 all-reduce.19
  398.0 111.9 all-reduce.21
  513.4 94.3 all-reduce.37
  619.5 96.4 all-reduce.23
  728.4 111.9 all-reduce.25
  843.9 93.4 all-reduce.27
  1003.8 96.3 all-reduce.29
  1110.5 111.9 all-reduce.31
  1226.0 94.3 all-reduce.35
  1332.2 96.3 all-reduce.33
where the time goes:
time: 1460 us; the launch traced here: 1450 us
  waiting for transfers between devices  1200 us (82%)
  other arithmetic  127 us (9%)
  matrix products  76.8 us (5%)
  local copies, waits for them, and re-layouts  27.8 us (2%)
  between operations  17.7 us (1%)
    psum x6, waiting for transfers between devices, from_root(): return lax.psum(jnp.where(mine, array, jnp.zeros_like(array)), axis)  608 us
    psum x4, waiting for transfers between devices, prepare(): gram, top_block = lax.psum((matmul(panel.T, panel), top_block), 'row')  374 us
    psum x2, waiting for transfers between devices, finish(): x_rows = lax.psum(matmul(matrix, w_cols), 'col')  218 us
    another operation x14, other arithmetic, prepare(): lower_factor = jnp.linalg.cholesky(gram)  69.3 us
    dot_general x40, matrix products, matmul(): jnp.dot(left, right, precision=lax.Precision.HIGHEST, preferred_element_t...  66.8 us
    another operation x3, other arithmetic, prepare(): jax.scipy.linalg.solve_triangular(lower_factor, panel.T, lower=True)  39.4 us
  transfers between devices with their start and end apart: 12, of which 12 were waited for; matrix products, arithmetic and copies ran while one was open for 1% of the time, Pallas kernels for 0%

commit v1 on v0

v1 whole, which is shorter than its diff:
```python
import functools
import math

import jax
import jax.numpy as jnp
from jax import lax
from jax.experimental import pallas as pl
from jax.experimental.pallas import tpu as pltpu
from jax.sharding import PartitionSpec as P

B = 256
F32 = jnp.float32
HIGH = lax.Precision.HIGH
HIGHEST = lax.Precision.HIGHEST
NN = (((1,), (0,)), ((), ()))
NT = (((1,), (1,)), ((), ()))
TN = (((0,), (0,)), ((), ()))


def dot(left, right, dims=NN, precision=HIGH):
    return lax.dot_general(left, right, dims, precision=precision, preferred_element_type=F32)


class Place:
    def __init__(self):
        self.row = lax.axis_index("row")
        self.col = lax.axis_index("col")
        self.x, self.y = self.row // 4, lax.rem(self.row, 4)
        self.z, self.core = self.col // 2, lax.rem(self.col, 2)
        self.slot = self.core * 8 + self.z

    def z_peer(self, d):
        return (self.row, lax.rem(self.z + d, 8) * 2 + self.core)

    def z_slot_to(self, d):
        return self.core * 8 + lax.rem(self.z + d, 8)

    def z_slot_from(self, d):
        return self.core * 8 + lax.rem(self.z + 8 - d, 8)

    def sibling(self):
        return (self.row, self.col + 1 - 2 * self.core)

    def col_peer(self, t):
        return (self.row, lax.rem(self.col + t, 16))

    def col_slot_to(self, t):
        other = lax.rem(self.col + t, 16)
        return lax.rem(other, 2) * 8 + other // 2

    def row_peer(self, d):
        return (self.row_to(d), self.col)

    def row_to(self, d):
        return lax.rem(self.x + d // 4, 4) * 4 + lax.rem(self.y + lax.rem(d, 4), 4)

    def row_from(self, d):
        return lax.rem(self.x + 4 - d // 4, 4) * 4 + lax.rem(self.y + 4 - lax.rem(d, 4), 4)


def loop(start, stop, body):
    def step(i, carry):
        body(i)
        return carry

    lax.fori_loop(start, stop, step, 0)


class Comm:
    def __init__(self, place, send, recv):
        self.at = place
        self.send = send
        self.recv = recv
        self.used = 0
        self.sent = []

    def take(self, count):
        base = self.used
        self.used += count
        return base

    def copy(self, src, dst, send_index, recv_index, device):
        return pltpu.make_async_remote_copy(
            src_ref=src,
            dst_ref=dst,
            send_sem=self.send.at[send_index],
            recv_sem=self.recv.at[recv_index],
            device_id=device,
            device_id_type=pl.DeviceIdType.MESH,
        )

    def finish(self):
        for wait in self.sent:
            wait()


class Exchange:
    def __init__(self, comm, first, stop, peer, src, dst, landed):
        self.comm, self.first, self.stop = comm, first, stop
        self.peer, self.src, self.dst, self.landed = peer, src, dst, landed
        self.base = comm.take(stop - first) - first
        comm.sent.append(self.wait_sends)

    def start_one(self, d):
        i = self.base + d
        self.comm.copy(self.src(d), self.dst(d), i, i, self.peer(d)).start()

    def start(self):
        loop(self.first, self.stop, self.start_one)

    def wait_one(self, d):
        i = self.base + d
        self.comm.copy(self.landed(d), self.landed(d), i, i, self.peer(d)).wait_recv()

    def wait(self):
        loop(self.first, self.stop, self.wait_one)

    def wait_sends(self):
        def one(d):
            i = self.base + d
            self.comm.copy(self.src(d), self.dst(d), i, i, self.peer(d)).wait_send()

        loop(self.first, self.stop, one)


class Deal:
    def __init__(self, comm, source, peer, src, dst, landed):
        self.comm, self.source = comm, source
        self.peer, self.src, self.dst, self.landed = peer, src, dst, landed
        self.base = comm.take(16)
        comm.sent.append(self.wait_sends)

    def copy(self, t):
        return self.comm.copy(self.src(t), self.dst(t), self.base + t, self.base, self.peer(t))

    def start(self):
        @pl.when(self.source)
        def _():
            loop(1, 16, lambda t: self.copy(t).start())

    def wait(self):
        @pl.when(jnp.logical_not(self.source))
        def _():
            self.comm.copy(self.landed, self.landed, self.base, self.base, self.peer(1)).wait_recv()

    def wait_sends(self):
        @pl.when(self.source)
        def _():
            loop(1, 16, lambda t: self.copy(t).wait_send())


class GatherCol:
    def __init__(self, comm, part):
        at = comm.at
        self.at = at
        self.z = Exchange(
            comm, 1, 8, at.z_peer, lambda d: part(at.slot), lambda d: part(at.slot), lambda d: part(at.z_slot_from(d))
        )
        sibling = lambda d: at.sibling()
        other = lambda d: (1 - at.core) * 8 + lax.rem(at.z + 8 - d, 8)
        self.pair = Exchange(
            comm, 0, 8, sibling, lambda d: part(at.z_slot_from(d)), lambda d: part(at.z_slot_from(d)),
            lambda d: part(other(d)),
        )

    def start(self):
        self.z.start()
        self.pair.start_one(0)

    def forward(self):
        def one(d):
            self.z.wait_one(d)
            self.pair.start_one(d)

        loop(1, 8, one)

    def wait(self):
        self.pair.wait()


def cholesky_strips(aug, first, stop):
    sub = lax.broadcasted_iota(jnp.int32, (8, 128), 0)
    lane = lax.broadcasted_iota(jnp.int32, (8, B), 1)

    def strip(s):
        rows = pl.ds(pl.multiple_of(8 * s, 8), 8)
        diag = aug[rows, pl.ds(pl.multiple_of((s // 16) * 128, 128), 128)]
        diag = pltpu.roll(diag, lax.rem(128 - 8 * lax.rem(s, 16), 128), 1)
        parts = [aug[rows, 128 * k : 128 * k + 128] for k in range(4)]
        cols = [jnp.broadcast_to(diag[:, j : j + 1], (8, 128)) for j in range(8)]
        pivots = jnp.ones((8, 128), F32)
        for j in range(8):
            pivot = jnp.broadcast_to(cols[j][j : j + 1, :], (8, 128))
            pivots = jnp.where(sub == j, pivot, pivots)
            scale = jnp.where(sub > j, cols[j] / pivot, 0.0)
            for k in range(j + 1, 8):
                cols[k] = cols[k] - scale * jnp.broadcast_to(cols[k][j : j + 1, :], (8, 128))
            for k in range(4):
                parts[k] = parts[k] - scale * jnp.broadcast_to(parts[k][j : j + 1, :], (8, 128))
        norm = 1.0 / jnp.sqrt(pivots)
        parts = [part * norm for part in parts]
        whole = jnp.concatenate(parts, axis=1)
        left = jnp.where(lane >= 8 * (s + 1), whole[:, :B], 0.0)
        aug[...] = aug[...] - dot(left.T, whole, NN, HIGHEST)
        aug[rows, :] = whole

    loop(first, stop, strip)


def kernel(a_ref, out_ref, band_ref, g, stage_r, stage_c, pr, pc, er, ec, prt, ypr, ypc, half, zr, xr, yr, yc,
           gx, sm1, sm2, aug, left, right, small, local_sem, send_sem, recv_sem):
    at = Place()
    comm = Comm(at, send_sem, recv_sem)
    row, col, slot = at.row, at.col, at.slot
    load = pltpu.make_async_copy(a_ref, g, local_sem.at[0])
    load.start()
    barrier = pltpu.get_barrier_semaphore()

    def greet(t):
        pl.semaphore_signal(barrier, inc=1, device_id=at.col_peer(t), device_id_type=pl.DeviceIdType.MESH)
        pl.semaphore_signal(barrier, inc=1, device_id=at.row_peer(t), device_id_type=pl.DeviceIdType.MESH)

    loop(1, 16, greet)
    load.wait()
    pl.semaphore_wait(barrier, 30)

    def rows64(ref, s):
        return ref.at[pl.ds(pl.multiple_of(64 * s, 64), 64)]

    def rows16(ref, s):
        return ref.at[pl.ds(pl.multiple_of(16 * s, 16), 16)]

    class Spread:
        def __init__(self, b, to_r, to_c):
            self.b, self.to_r, self.to_c = b, to_r, to_c
            self.deal_r = Deal(
                comm, col == b, at.col_peer,
                lambda t: rows64(stage_r, at.col_slot_to(t)), lambda t: rows64(to_r, at.col_slot_to(t)),
                rows64(to_r, slot),
            )
            self.deal_c = Deal(
                comm, row == b, at.row_peer,
                lambda t: rows16(stage_c, at.row_to(t)), lambda t: rows16(to_c, at.row_to(t)), rows16(to_c, row),
            )
            self.gather_r = GatherCol(comm, lambda s: rows64(to_r, s))
            self.gather_c = Exchange(
                comm, 1, 16, at.row_peer, lambda d: rows16(to_c, row), lambda d: rows16(to_c, row),
                lambda d: rows16(to_c, at.row_from(d)),
            )

        def deal(self, masked):
            @pl.when(col == self.b)
            def _():
                stage_r[...] = g[:, 0:B]
                if masked:
                    @pl.when(row == 0)
                    def _():
                        stage_r[0:B, :] = jnp.zeros((B, B), F32)
                mine = pl.ds(pl.multiple_of(64 * slot, 64), 64)
                self.to_r[mine, :] = stage_r[mine, :]

            self.deal_r.start()

            @pl.when(row == self.b)
            def _():
                stage_c[...] = g[0:B, :]
                if masked:
                    @pl.when(col == 0)
                    def _():
                        stage_c[:, 0:B] = jnp.zeros((B, B), F32)
                mine = pl.ds(pl.multiple_of(16 * row, 16), 16)
                self.to_c[mine, :] = stage_c[mine, :]

            self.deal_c.start()

        def gather(self):
            self.deal_r.wait()
            self.gather_r.start()
            self.deal_c.wait()
            self.gather_c.start()

        def forward(self):
            self.gather_r.forward()

        def wait(self):
            self.gather_r.wait()
            self.gather_c.wait()

    def panel(p, spread_e):
        panel_r, panel_c, side_r, side_c = pr.at[p], pc.at[p], er.at[p], ec.at[p]
        top = p + 1
        sums1, sums2, full_r, full_c = sm1.at[p], sm2.at[p], yr.at[p], yc.at[p]
        mine16 = pl.ds(pl.multiple_of(16 * slot, 16), 16)

        def small_sum(which, sums, value, rows):
            own, got = gx.at[p, which, 0], gx.at[p, which]
            own[...] = value
            ring = Exchange(comm, 1, 16, at.row_peer, lambda d: own, lambda d: got.at[d], lambda d: got.at[d])
            ring.start()
            tops = sums.at[slot, pl.ds(16, rows - 16)]
            deal = Deal(comm, row == top, at.row_peer, lambda t: tops, lambda t: tops, tops)
            gather = GatherCol(comm, lambda s: sums.at[s])
            return ring, got, deal, gather

        def small_finish(parts, sums):
            ring, got, deal, gather = parts
            ring.wait()
            total = got[0]
            for d in range(1, 16):
                total = total + got[d]
            sums[slot, 0:16, :] = total
            deal.wait()
            gather.start()

        prt[...] = panel_r[...].T
        gram_parts = small_sum(0, sums1, dot(prt[mine16, :], panel_r[...], NN, HIGHEST), 32)

        @pl.when(row == top)
        def _():
            sums1[slot, 16:32, :] = panel_r[mine16, :]

        gram_parts[2].start()

        if p == 1:
            def update(n):
                lanes = pl.ds(pl.multiple_of(n * B, B), B)
                g[:, lanes] = g[:, lanes] - dot(left[...], right[:, lanes])

            loop(0, 4, update)
            spread_e.deal(False)

        pair = Exchange(
            comm, 0, 1, lambda d: at.sibling(),
            lambda d: ypr.at[p, pl.ds(pl.multiple_of(512 * (1 - at.core), 512), 512)], lambda d: half.at[p],
            lambda d: half.at[p],
        )
        cross = Exchange(
            comm, 1, 8, at.z_peer, lambda d: rows64(ypr.at[p], at.z_slot_to(d)), lambda d: zr.at[p, d],
            lambda d: zr.at[p, d],
        )
        ring = Exchange(
            comm, 1, 16, at.row_peer, lambda d: rows16(ypc.at[p], at.row_to(d)), lambda d: xr.at[p, d],
            lambda d: xr.at[p, d],
        )

        def product_rows(base, m):
            rows = pl.ds(pl.multiple_of(base + m * B, B), B)
            ypr[p, rows, :] = dot(g[rows, :], panel_c[...], NT)

        def product_cols(n):
            lanes = pl.ds(pl.multiple_of(n * B, B), B)
            ypc[p, :, lanes] = dot(prt[...], g[:, lanes])

        loop(0, 2, lambda m: product_rows(512 * (1 - at.core), m))
        pair.start()
        loop(0, 2, lambda m: product_rows(512 * at.core, m))
        pair.wait()
        mine512 = pl.ds(pl.multiple_of(512 * at.core, 512), 512)
        ypr[p, mine512, :] = ypr[p, mine512, :] + half[p]
        cross.start()
        loop(0, 4, product_cols)
        ring.start()

        small_finish(gram_parts, sums1)
        if p == 1:
            spread_e.gather()
        else:
            spread_e.forward()
        gram_parts[3].forward()
        gram_parts[3].wait()

        eye = (lax.broadcasted_iota(jnp.int32, (B, B), 0) == lax.broadcasted_iota(jnp.int32, (B, B), 1)).astype(F32)
        aug[:, 0:B] = sums1[:, 0:16, :].reshape(B, B)
        aug[:, B : 2 * B] = eye
        cholesky_strips(aug, 0, 16)

        cross.wait()
        mine64 = pl.ds(pl.multiple_of(64 * slot, 64), 64)
        total = ypr[p, mine64, :]
        for d in range(1, 8):
            total = total + zr[p, d]
        full_r[mine64, :] = total
        gather_r = GatherCol(comm, lambda s: rows64(full_r, s))
        gather_r.start()
        ring.wait()
        own16 = pl.ds(pl.multiple_of(16 * row, 16), 16)
        total = ypc[p, own16, :]
        for d in range(1, 16):
            total = total + xr[p, d]
        full_c[own16, :] = total
        gather_c = Exchange(
            comm, 1, 16, at.row_peer, lambda d: rows16(full_c, row), lambda d: rows16(full_c, row),
            lambda d: rows16(full_c, at.row_from(d)),
        )
        gather_c.start()

        cholesky_strips(aug, 16, 32)
        upper = jnp.where(
            lax.broadcasted_iota(jnp.int32, (B, B), 1) >= lax.broadcasted_iota(jnp.int32, (B, B), 0), aug[:, 0:B], 0.0
        )
        band_ref[p] = upper / 128.0
        inverse = aug[:, B : 2 * B]
        panel_top = sums1[:, 16:32, :].reshape(B, B)
        c_top = dot(panel_top, inverse, NT, HIGHEST)
        power = dot(inverse, panel_top, NT, HIGHEST)
        inverse_t = eye + power
        for _ in range(5):
            power = dot(power, power, NN, HIGHEST)
            inverse_t = inverse_t + dot(inverse_t, power, NN, HIGHEST)

        if p == 1:
            spread_e.forward()
        gather_r.forward()
        gather_r.wait()
        middle_parts = small_sum(1, sums2, dot(prt[mine16, :], full_r[...], NN, HIGHEST), 48)
        spread_e.wait()

        @pl.when(row == top)
        def _():
            sums2[slot, 16:32, :] = full_r[mine16, :]
            sums2[slot, 32:48, :] = side_r[mine16, :]

        middle_parts[2].start()

        def w_and_x_rows(m):
            rows = pl.ds(pl.multiple_of(m * B, B), B)
            left[rows, 0:B] = -dot(panel_r[rows, :], inverse, NT)
            left[rows, B : 2 * B] = dot(side_r[rows, :] - dot(full_r[rows, :], inverse, NT), inverse_t)

        loop(0, 4, w_and_x_rows)

        @pl.when(row == top)
        def _():
            left[0:B, 0:B] = left[0:B, 0:B] + eye

        gather_c.wait()

        def w_and_x_cols(n):
            lanes = pl.ds(pl.multiple_of(n * B, B), B)
            right[B : 2 * B, lanes] = -dot(inverse, panel_c[:, lanes])
            right[0:B, lanes] = dot(inverse_t, side_c[:, lanes] - dot(inverse, full_c[:, lanes]), TN)

        loop(0, 4, w_and_x_cols)

        @pl.when(col == top)
        def _():
            right[B : 2 * B, 0:B] = right[B : 2 * B, 0:B] + eye

        small_finish(middle_parts, sums2)
        middle_parts[3].forward()
        middle_parts[3].wait()
        inner = sums2[:, 0:16, :].reshape(B, B)
        y_top = sums2[:, 16:32, :].reshape(B, B)
        e_top = sums2[:, 32:48, :].reshape(B, B)
        middle = (
            e_top
            - dot(y_top, inverse, NT, HIGHEST)
            - dot(inverse, y_top, NT, HIGHEST)
            + dot(dot(inverse, inner, NN, HIGHEST), inverse, NT, HIGHEST)
        )
        sym = dot(inverse_t, dot(middle, inverse_t, NN, HIGHEST), TN, HIGHEST)
        half_sym = 0.5 * sym

        def u_rows(m):
            rows = pl.ds(pl.multiple_of(m * B, B), B)
            left[rows, B : 2 * B] = left[rows, B : 2 * B] - dot(left[rows, 0:B], half_sym)

        loop(0, 4, u_rows)

        def u_cols(n):
            lanes = pl.ds(pl.multiple_of(n * B, B), B)
            right[0:B, lanes] = right[0:B, lanes] - dot(half_sym, right[B : 2 * B, lanes], TN)

        loop(0, 4, u_cols)
        if p == 1:
            return
        w_top = eye - c_top
        x_top = e_top - dot(y_top, inverse, NT, HIGHEST)
        u_top = dot(x_top, inverse_t, NN, HIGHEST) - dot(w_top, half_sym, NN, HIGHEST)
        small[0] = w_top
        small[1] = u_top

        def next_rows(m):
            rows = pl.ds(pl.multiple_of(m * B, B), B)
            pr[1, rows, :] = (
                side_r[rows, :]
                - dot(left[rows, 0:B], small[1], NT)
                - dot(left[rows, B : 2 * B], small[0], NT)
            )

        loop(0, 4, next_rows)

        @pl.when(row < 2)
        def _():
            pr[1, 0:B, :] = jnp.zeros((B, B), F32)

        def next_cols(n):
            lanes = pl.ds(pl.multiple_of(n * B, B), B)
            pc[1, :, lanes] = (
                side_c[:, lanes] - dot(small[1], right[B : 2 * B, lanes]) - dot(small[0], right[0:B, lanes])
            )

        loop(0, 4, next_cols)

        @pl.when(col < 2)
        def _():
            pc[1, :, 0:B] = jnp.zeros((B, B), F32)

    spread_p = Spread(0, pr.at[0], pc.at[0])
    spread_e = Spread(1, er.at[0], ec.at[0])
    spread_p.deal(True)
    spread_e.deal(False)
    spread_p.gather()
    spread_e.gather()
    spread_p.forward()
    spread_p.wait()
    panel(0, spread_e)
    panel(1, Spread(2, er.at[1], ec.at[1]))

    def last(n):
        lanes = pl.ds(pl.multiple_of(n * B, B), B)
        g[:, lanes] = g[:, lanes] - dot(left[...], right[:, lanes])

        @pl.when(row < 2)
        def _():
            g[0:B, lanes] = jnp.zeros((B, B), F32)

        @pl.when(jnp.logical_and(col < 2, n == 0))
        def _():
            g[:, lanes] = jnp.zeros((4 * B, B), F32)

        pltpu.make_async_copy(g.at[:, lanes], out_ref.at[:, lanes], local_sem.at[n]).start()

    loop(0, 4, last)
    comm.finish()

    def drain(n):
        lanes = pl.ds(pl.multiple_of(n * B, B), B)
        pltpu.make_async_copy(g.at[:, lanes], out_ref.at[:, lanes], local_sem.at[n]).wait()

    loop(0, 4, drain)


def shards(matrix_cyclic):
    vmem = lambda *shape: pltpu.VMEM(shape, F32)
    return pl.pallas_call(
        kernel,
        out_shape=(
            jax.ShapeDtypeStruct((1024, 1024), F32),
            jax.ShapeDtypeStruct((2, B, B), F32),
        ),
        in_specs=[pl.BlockSpec(memory_space=pl.ANY)],
        out_specs=(pl.BlockSpec(memory_space=pl.ANY), pl.BlockSpec(memory_space=pltpu.VMEM)),
        scratch_shapes=[
            vmem(1024, 1024),
            vmem(1024, B), vmem(B, 1024),
            vmem(2, 1024, B), vmem(2, B, 1024),
            vmem(2, 1024, B), vmem(2, B, 1024),
            vmem(B, 1024),
            vmem(2, 1024, B), vmem(2, B, 1024),
            vmem(2, 512, B), vmem(2, 8, 64, B), vmem(2, 16, 16, 1024),
            vmem(2, 1024, B), vmem(2, B, 1024),
            vmem(2, 2, 16, 16, B), vmem(2, 16, 32, B), vmem(2, 16, 48, B),
            vmem(B, 2 * B),
            vmem(1024, 2 * B), vmem(2 * B, 1024),
            vmem(2, B, B),
            pltpu.SemaphoreType.DMA((4,)),
            pltpu.SemaphoreType.DMA((480,)),
            pltpu.SemaphoreType.DMA((480,)),
        ],
        compiler_params=pltpu.CompilerParams(
            collective_id=0, has_side_effects=True, vmem_limit_bytes=60 * 1024 * 1024
        ),
    )(matrix_cyclic)


def solution(mesh):
    return jax.shard_map(
        shards,
        mesh=mesh,
        in_specs=(P("row", "col"),),
        out_specs=(P("row", "col"), P()),
        check_vma=False,
    )
```

time: 1460 us -> 255 us (0.17)
  waiting for transfers between devices: 1200 us -> 0 us
  Pallas kernels: 0 us -> 248 us
  other arithmetic: 127 us -> 0 us
  matrix products: 76.8 us -> 0 us
  local copies, waits for them, and re-layouts: 27.8 us -> 5.64 us
  between operations: 17.7 us -> 0.65 us
    psum x12 -> x0, waiting for transfers between devices: 1200 us -> none  [the longest x6 608 us: from_root(): return lax.psum(jnp.where(mine, array, jnp.zeros_like(array)), axis)]
    pallas_call x0 -> x1, Pallas kernels: none -> 248 us  [shards(): pl.pallas_call(kernel, out_shape=(jax.ShapeDtypeStruct((1024, 1024), F32)...]
    another operation x19 -> x0, other arithmetic: 110 us -> none  [the longest x14 69.3 us: prepare(): lower_factor = jnp.linalg.cholesky(gram)]
    dot_general x40 -> x0, matrix products: 66.8 us -> none  [matmul(): jnp.dot(left, right, precision=lax.Precision.HIGHEST, preferred_element_t...]
  transfers between devices with their start and end apart: 12 -> 0, of which waited for: 12 -> 0; matrix products, arithmetic and copies ran while one was open for 1% -> 0% of each run, Pallas kernels for 0% -> 0%
where the time goes in v1:
time: 255 us
  Pallas kernels  248 us (97%)
  local copies, waits for them, and re-layouts  5.64 us (2%)
    pallas_call x1, Pallas kernels, shards(): pl.pallas_call(kernel, out_shape=(jax.ShapeDtypeStruct((1024, 1024), F32)...  248 us
    unnamed x4, local copies, waits for them, and re-layouts  5.64 us

profile of v1, /device:TPU:1, one launch (start us, length us, event | category | flops | bytes accessed | tf_op | source)
XLA Modules:
  0.0 254.8 jit_solution(6477385341303450983)
XLA Ops:
  0.6 248.5 %shard_map.30 = (f32[1024,1024]{1,0:T(8,128)}, f32[2,256,256]{2,1,0:T(8,128)}) custom-call(f32[1024,1024]{1,0:T(8,128)} %a_ref.1), custom_call_target="tpu_custom_call" | custom-call | tf_op jit(solution)/shard_map/pallas_call | solution.py:546
  249.1 0.0 copy-start
  249.1 4.8 %copy.5 = f32[1024,1024]{1,0:T(8,128)} copy(f32[1024,1024]{1,0:T(8,128)} %get-tuple-element.4) | data formatting | bytes 8388608
  254.0 0.0 copy-done
  254.0 0.8 copy.6
Async XLA Ops:
  249.1 4.9 %copy-start = (f32[2,256,256]{2,1,0:T(8,128)S(1)}, f32[2,256,256]{2,1,0:T(8,128)}, u32[]{:S(2)}) copy-start(f32[2,256,256]{2,1,0:T(8,128)} %get-tuple-element.5) | copy-start | bytes 1572868

commit v2 on v1

--- a/solution.py
+++ b/solution.py
@@ -178,37 +178,52 @@
         self.pair.wait()
 
 
-def cholesky_strips(aug, first, stop):
+def cholesky_block(aug, block):
     sub = lax.broadcasted_iota(jnp.int32, (8, 128), 0)
-    lane = lax.broadcasted_iota(jnp.int32, (8, B), 1)
-
-    def strip(s):
-        rows = pl.ds(pl.multiple_of(8 * s, 8), 8)
-        diag = aug[rows, pl.ds(pl.multiple_of((s // 16) * 128, 128), 128)]
-        diag = pltpu.roll(diag, lax.rem(128 - 8 * lax.rem(s, 16), 128), 1)
+    lane = lax.broadcasted_iota(jnp.int32, (8, 128), 1)
+    base = 64 * block
+    first = 128 * (base // 128)
+    offset = base - first
+
+    def strip(i):
+        rows = pl.ds(pl.multiple_of(base + 8 * i, 8), 8)
+        diag = pltpu.roll(aug[rows, first : first + 128], lax.rem(128 - offset - 8 * i, 128), 1)
         parts = [aug[rows, 128 * k : 128 * k + 128] for k in range(4)]
         cols = [jnp.broadcast_to(diag[:, j : j + 1], (8, 128)) for j in range(8)]
         pivots = jnp.ones((8, 128), F32)
         for j in range(8):
             pivot = jnp.broadcast_to(cols[j][j : j + 1, :], (8, 128))
             pivots = jnp.where(sub == j, pivot, pivots)
-            scale = jnp.where(sub > j, cols[j] / pivot, 0.0)
+            scale = jnp.where(sub > j, cols[j] * (1.0 / pivot), 0.0)
             for k in range(j + 1, 8):
                 cols[k] = cols[k] - scale * jnp.broadcast_to(cols[k][j : j + 1, :], (8, 128))
             for k in range(4):
                 parts[k] = parts[k] - scale * jnp.broadcast_to(parts[k][j : j + 1, :], (8, 128))
         norm = 1.0 / jnp.sqrt(pivots)
         parts = [part * norm for part in parts]
-        whole = jnp.concatenate(parts, axis=1)
-        left = jnp.where(lane >= 8 * (s + 1), whole[:, :B], 0.0)
-        aug[...] = aug[...] - dot(left.T, whole, NN, HIGHEST)
-        aug[rows, :] = whole
-
-    loop(first, stop, strip)
+        factors = jnp.where(lane >= offset + 8 * (i + 1), parts[first // 128], 0.0).T
+        for t in range(8):
+            below = slice(base + 8 * t, base + 8 * t + 8)
+            spread = [
+                jnp.broadcast_to(factors[offset + 8 * t : offset + 8 * t + 8, j : j + 1], (8, 128)) for j in range(8)
+            ]
+            for k in range(4):
+                lanes = slice(128 * k, 128 * k + 128)
+                rest = aug[below, lanes]
+                for j in range(8):
+                    rest = rest - spread[j] * jnp.broadcast_to(parts[k][j : j + 1, :], (8, 128))
+                aug[below, lanes] = rest
+        for k in range(4):
+            aug[rows, 128 * k : 128 * k + 128] = parts[k]
+
+    loop(0, 8, strip)
+    if base + 64 < B:
+        done = aug[base : base + 64, :]
+        aug[base + 64 :, :] = aug[base + 64 :, :] - dot(done[:, base + 64 : B], done, TN, HIGHEST)
 
 
 def kernel(a_ref, out_ref, band_ref, g, stage_r, stage_c, pr, pc, er, ec, prt, ypr, ypc, half, zr, xr, yr, yc,
-           gx, sm1, sm2, aug, left, right, small, local_sem, send_sem, recv_sem):
+           gx, sm1, sm2, top1, top2, aug, left, right, small, local_sem, send_sem, recv_sem):
     at = Place()
     comm = Comm(at, send_sem, recv_sem)
     row, col, slot = at.row, at.col, at.slot
@@ -286,42 +301,52 @@
             self.gather_r.wait()
             self.gather_c.wait()
 
-    def panel(p, spread_e):
+    def panel(p, spread_e, tops1):
         panel_r, panel_c, side_r, side_c = pr.at[p], pc.at[p], er.at[p], ec.at[p]
         top = p + 1
-        sums1, sums2, full_r, full_c = sm1.at[p], sm2.at[p], yr.at[p], yc.at[p]
+        full_r, full_c = yr.at[p], yc.at[p]
         mine16 = pl.ds(pl.multiple_of(16 * slot, 16), 16)
-
-        def small_sum(which, sums, value, rows):
-            own, got = gx.at[p, which, 0], gx.at[p, which]
-            own[...] = value
-            ring = Exchange(comm, 1, 16, at.row_peer, lambda d: own, lambda d: got.at[d], lambda d: got.at[d])
-            ring.start()
-            tops = sums.at[slot, pl.ds(16, rows - 16)]
-            deal = Deal(comm, row == top, at.row_peer, lambda t: tops, lambda t: tops, tops)
+        own16 = pl.ds(pl.multiple_of(16 * row, 16), 16)
+        mine64 = pl.ds(pl.multiple_of(64 * slot, 64), 64)
+        mine8 = pl.ds(pl.multiple_of(8 * at.core, 8), 8)
+
+        def row_sum(which, sums):
+            got = gx.at[p, which]
+            ring = Exchange(comm, 1, 16, at.row_peer, lambda d: got.at[0], lambda d: got.at[d], lambda d: got.at[d])
             gather = GatherCol(comm, lambda s: sums.at[s])
-            return ring, got, deal, gather
-
-        def small_finish(parts, sums):
-            ring, got, deal, gather = parts
-            ring.wait()
-            total = got[0]
-            for d in range(1, 16):
-                total = total + got[d]
-            sums[slot, 0:16, :] = total
-            deal.wait()
-            gather.start()
+
+            def begin(value):
+                got[0] = value
+                ring.start()
+
+            def reduce():
+                ring.wait()
+                total = got[0]
+                for d in range(1, 16):
+                    total = total + got[d]
+                sums[slot] = total
+                gather.start()
+
+            def end():
+                gather.forward()
+                gather.wait()
+
+            return begin, reduce, end
+
+        gram_begin, gram_reduce, gram_end = row_sum(0, sm1.at[p])
+        inner_begin, inner_reduce, inner_end = row_sum(1, sm2.at[p])
+        tops2 = Tops(top, top2.at[p])
 
         prt[...] = panel_r[...].T
-        gram_parts = small_sum(0, sums1, dot(prt[mine16, :], panel_r[...], NN, HIGHEST), 32)
-
-        @pl.when(row == top)
-        def _():
-            sums1[slot, 16:32, :] = panel_r[mine16, :]
-
-        gram_parts[2].start()
+        gram_begin(dot(prt[mine16, :], panel_r[...], NN, HIGHEST))
 
         if p == 1:
+            @pl.when(col == top)
+            def _():
+                top1[p, row] = panel_c[own16, 0:B]
+
+            tops1.deal.start()
+
             def update(n):
                 lanes = pl.ds(pl.multiple_of(n * B, B), B)
                 g[:, lanes] = g[:, lanes] - dot(left[...], right[:, lanes])
@@ -331,161 +356,161 @@
 
         pair = Exchange(
             comm, 0, 1, lambda d: at.sibling(),
-            lambda d: ypr.at[p, pl.ds(pl.multiple_of(512 * (1 - at.core), 512), 512)], lambda d: half.at[p],
+            lambda d: ypr.at[p, pl.ds(pl.multiple_of(8 * (1 - at.core), 8), 8)], lambda d: half.at[p],
             lambda d: half.at[p],
         )
         cross = Exchange(
-            comm, 1, 8, at.z_peer, lambda d: rows64(ypr.at[p], at.z_slot_to(d)), lambda d: zr.at[p, d],
-            lambda d: zr.at[p, d],
+            comm, 1, 8, at.z_peer, lambda d: ypr.at[p, at.z_slot_to(d)], lambda d: zr.at[p, d], lambda d: zr.at[p, d]
         )
         ring = Exchange(
             comm, 1, 16, at.row_peer, lambda d: rows16(ypc.at[p], at.row_to(d)), lambda d: xr.at[p, d],
             lambda d: xr.at[p, d],
         )
 
-        def product_rows(base, m):
-            rows = pl.ds(pl.multiple_of(base + m * B, B), B)
-            ypr[p, rows, :] = dot(g[rows, :], panel_c[...], NT)
+        def product_rows(m):
+            rows = pl.ds(pl.multiple_of(m * B, B), B)
+            value = dot(g[rows, :], panel_c[...], NT)
+            ypr[p, pl.ds(pl.multiple_of(4 * m, 4), 4), 0:64, :] = value.reshape(4, 64, B)
 
         def product_cols(n):
             lanes = pl.ds(pl.multiple_of(n * B, B), B)
             ypc[p, :, lanes] = dot(prt[...], g[:, lanes])
 
-        loop(0, 2, lambda m: product_rows(512 * (1 - at.core), m))
+        loop(0, 4, product_rows)
+        ypr[p, :, 64:80, :] = dot(prt[...], ypr[p, :, 0:64, :].reshape(4 * B, B)).reshape(16, 16, B)
         pair.start()
-        loop(0, 2, lambda m: product_rows(512 * at.core, m))
+        loop(0, 2, product_cols)
+        gram_reduce()
         pair.wait()
-        mine512 = pl.ds(pl.multiple_of(512 * at.core, 512), 512)
-        ypr[p, mine512, :] = ypr[p, mine512, :] + half[p]
+        ypr[p, mine8] = ypr[p, mine8] + half[p]
         cross.start()
-        loop(0, 4, product_cols)
+        loop(2, 4, product_cols)
         ring.start()
-
-        small_finish(gram_parts, sums1)
-        if p == 1:
+        if p == 0:
+            spread_e.forward()
+        else:
+            tops1.gather()
             spread_e.gather()
-        else:
-            spread_e.forward()
-        gram_parts[3].forward()
-        gram_parts[3].wait()
-
+
+        gram_end()
         eye = (lax.broadcasted_iota(jnp.int32, (B, B), 0) == lax.broadcasted_iota(jnp.int32, (B, B), 1)).astype(F32)
-        aug[:, 0:B] = sums1[:, 0:16, :].reshape(B, B)
+        aug[:, 0:B] = sm1[p].reshape(B, B)
         aug[:, B : 2 * B] = eye
-        cholesky_strips(aug, 0, 16)
-
+        cholesky_block(aug, 0)
+
+        gather_r = GatherCol(comm, lambda s: rows64(full_r, s))
+        gather_c = Exchange(
+            comm, 1, 16, at.row_peer, lambda d: rows16(full_c, row), lambda d: rows16(full_c, row),
+            lambda d: rows16(full_c, at.row_from(d)),
+        )
         cross.wait()
-        mine64 = pl.ds(pl.multiple_of(64 * slot, 64), 64)
-        total = ypr[p, mine64, :]
+        total = ypr[p, slot]
         for d in range(1, 8):
             total = total + zr[p, d]
-        full_r[mine64, :] = total
-        gather_r = GatherCol(comm, lambda s: rows64(full_r, s))
+        inner_begin(total[64:80, :])
+        full_r[mine64, :] = total[0:64, :]
         gather_r.start()
         ring.wait()
-        own16 = pl.ds(pl.multiple_of(16 * row, 16), 16)
         total = ypc[p, own16, :]
         for d in range(1, 16):
             total = total + xr[p, d]
         full_c[own16, :] = total
-        gather_c = Exchange(
-            comm, 1, 16, at.row_peer, lambda d: rows16(full_c, row), lambda d: rows16(full_c, row),
-            lambda d: rows16(full_c, at.row_from(d)),
-        )
+
+        @pl.when(col == top)
+        def _():
+            top2[p, row, 0:16, :] = total[:, 0:B]
+            top2[p, row, 16:32, :] = side_c[own16, 0:B]
+
+        tops2.deal.start()
         gather_c.start()
-
-        cholesky_strips(aug, 16, 32)
+        cholesky_block(aug, 1)
+        inner_reduce()
+        tops2.gather()
+        cholesky_block(aug, 2)
+        cholesky_block(aug, 3)
+
         upper = jnp.where(
             lax.broadcasted_iota(jnp.int32, (B, B), 1) >= lax.broadcasted_iota(jnp.int32, (B, B), 0), aug[:, 0:B], 0.0
         )
         band_ref[p] = upper / 128.0
         inverse = aug[:, B : 2 * B]
-        panel_top = sums1[:, 16:32, :].reshape(B, B)
-        c_top = dot(panel_top, inverse, NT, HIGHEST)
-        power = dot(inverse, panel_top, NT, HIGHEST)
+        tops1.ring.wait()
+        c_t = dot(inverse, top1[p].reshape(B, B))
+        power = c_t
         inverse_t = eye + power
         for _ in range(5):
-            power = dot(power, power, NN, HIGHEST)
-            inverse_t = inverse_t + dot(inverse_t, power, NN, HIGHEST)
+            power = dot(power, power)
+            inverse_t = inverse_t + dot(inverse_t, power)
+        small[2] = inverse_t
+        small[3] = dot(inverse, inverse_t, TN)
+
+        def w_rows(m):
+            rows = pl.ds(pl.multiple_of(m * B, B), B)
+            left[rows, 0:B] = -dot(panel_r[rows, :], aug[:, B : 2 * B], NT)
+
+        def w_cols(n):
+            lanes = pl.ds(pl.multiple_of(n * B, B), B)
+            right[B : 2 * B, lanes] = -dot(aug[:, B : 2 * B], panel_c[:, lanes])
+
+        loop(0, 4, w_rows)
+        loop(0, 4, w_cols)
+
+        @pl.when(row == top)
+        def _():
+            left[0:B, 0:B] = left[0:B, 0:B] + eye
+
+        @pl.when(col == top)
+        def _():
+            right[B : 2 * B, 0:B] = right[B : 2 * B, 0:B] + eye
 
         if p == 1:
             spread_e.forward()
         gather_r.forward()
+        spread_e.wait()
         gather_r.wait()
-        middle_parts = small_sum(1, sums2, dot(prt[mine16, :], full_r[...], NN, HIGHEST), 48)
-        spread_e.wait()
-
-        @pl.when(row == top)
-        def _():
-            sums2[slot, 16:32, :] = full_r[mine16, :]
-            sums2[slot, 32:48, :] = side_r[mine16, :]
-
-        middle_parts[2].start()
-
-        def w_and_x_rows(m):
-            rows = pl.ds(pl.multiple_of(m * B, B), B)
-            left[rows, 0:B] = -dot(panel_r[rows, :], inverse, NT)
-            left[rows, B : 2 * B] = dot(side_r[rows, :] - dot(full_r[rows, :], inverse, NT), inverse_t)
-
-        loop(0, 4, w_and_x_rows)
-
-        @pl.when(row == top)
-        def _():
-            left[0:B, 0:B] = left[0:B, 0:B] + eye
-
-        gather_c.wait()
-
-        def w_and_x_cols(n):
-            lanes = pl.ds(pl.multiple_of(n * B, B), B)
-            right[B : 2 * B, lanes] = -dot(inverse, panel_c[:, lanes])
-            right[0:B, lanes] = dot(inverse_t, side_c[:, lanes] - dot(inverse, full_c[:, lanes]), TN)
-
-        loop(0, 4, w_and_x_cols)
-
-        @pl.when(col == top)
-        def _():
-            right[B : 2 * B, 0:B] = right[B : 2 * B, 0:B] + eye
-
-        small_finish(middle_parts, sums2)
-        middle_parts[3].forward()
-        middle_parts[3].wait()
-        inner = sums2[:, 0:16, :].reshape(B, B)
-        y_top = sums2[:, 16:32, :].reshape(B, B)
-        e_top = sums2[:, 32:48, :].reshape(B, B)
-        middle = (
-            e_top
-            - dot(y_top, inverse, NT, HIGHEST)
-            - dot(inverse, y_top, NT, HIGHEST)
-            + dot(dot(inverse, inner, NN, HIGHEST), inverse, NT, HIGHEST)
-        )
-        sym = dot(inverse_t, dot(middle, inverse_t, NN, HIGHEST), TN, HIGHEST)
-        half_sym = 0.5 * sym
 
         def u_rows(m):
             rows = pl.ds(pl.multiple_of(m * B, B), B)
-            left[rows, B : 2 * B] = left[rows, B : 2 * B] - dot(left[rows, 0:B], half_sym)
-
-        loop(0, 4, u_rows)
+            left[rows, B : 2 * B] = dot(side_r[rows, :], small[2]) - dot(full_r[rows, :], small[3])
 
         def u_cols(n):
             lanes = pl.ds(pl.multiple_of(n * B, B), B)
-            right[0:B, lanes] = right[0:B, lanes] - dot(half_sym, right[B : 2 * B, lanes], TN)
-
+            right[0:B, lanes] = dot(small[2], side_c[:, lanes], TN) - dot(small[3], full_c[:, lanes], TN)
+
+        loop(0, 4, u_rows)
+        gather_c.wait()
         loop(0, 4, u_cols)
+
+        inner_end()
+        tops2.ring.wait()
+        y_top = top2[p, :, 0:16, :].reshape(B, B)
+        e_top = top2[p, :, 16:32, :].reshape(B, B)
+        y_top = dot(inverse, y_top)
+        x_top = e_top - y_top.T
+        middle = x_top - y_top + dot(dot(inverse, sm2[p].reshape(B, B)), inverse, NT)
+        half_sym = 0.5 * dot(inverse_t, dot(middle, inverse_t), TN)
+        small[4] = half_sym
+
+        def end_rows(m):
+            rows = pl.ds(pl.multiple_of(m * B, B), B)
+            left[rows, B : 2 * B] = left[rows, B : 2 * B] - dot(left[rows, 0:B], small[4])
+
+        def end_cols(n):
+            lanes = pl.ds(pl.multiple_of(n * B, B), B)
+            right[0:B, lanes] = right[0:B, lanes] - dot(small[4], right[B : 2 * B, lanes], TN)
+
+        loop(0, 4, end_rows)
+        loop(0, 4, end_cols)
         if p == 1:
             return
-        w_top = eye - c_top
-        x_top = e_top - dot(y_top, inverse, NT, HIGHEST)
-        u_top = dot(x_top, inverse_t, NN, HIGHEST) - dot(w_top, half_sym, NN, HIGHEST)
-        small[0] = w_top
-        small[1] = u_top
+        w_top_t = eye - c_t
+        small[0] = w_top_t
+        small[1] = dot(x_top, inverse_t) - dot(w_top_t, half_sym, TN)
 
         def next_rows(m):
             rows = pl.ds(pl.multiple_of(m * B, B), B)
             pr[1, rows, :] = (
-                side_r[rows, :]
-                - dot(left[rows, 0:B], small[1], NT)
-                - dot(left[rows, B : 2 * B], small[0], NT)
+                side_r[rows, :] - dot(left[rows, 0:B], small[1], NT) - dot(left[rows, B : 2 * B], small[0])
             )
 
         loop(0, 4, next_rows)
@@ -497,7 +522,7 @@
         def next_cols(n):
             lanes = pl.ds(pl.multiple_of(n * B, B), B)
             pc[1, :, lanes] = (
-                side_c[:, lanes] - dot(small[1], right[B : 2 * B, lanes]) - dot(small[0], right[0:B, lanes])
+                side_c[:, lanes] - dot(small[1], right[B : 2 * B, lanes]) - dot(small[0], right[0:B, lanes], TN)
             )
 
         loop(0, 4, next_cols)
@@ -505,17 +530,37 @@
         @pl.when(col < 2)
         def _():
             pc[1, :, 0:B] = jnp.zeros((B, B), F32)
+
+    class Tops:
+        def __init__(self, source, slabs):
+            own = slabs.at[row]
+            self.deal = Deal(comm, col == source, at.col_peer, lambda t: own, lambda t: own, own)
+            self.ring = Exchange(
+                comm, 1, 16, at.row_peer, lambda d: own, lambda d: own, lambda d: slabs.at[at.row_from(d)]
+            )
+
+        def gather(self):
+            self.deal.wait()
+            self.ring.start()
 
     spread_p = Spread(0, pr.at[0], pc.at[0])
     spread_e = Spread(1, er.at[0], ec.at[0])
+    tops_first = Tops(1, top1.at[0])
     spread_p.deal(True)
     spread_e.deal(False)
     spread_p.gather()
+
+    @pl.when(col == 1)
+    def _():
+        top1[0, row] = pc[0, pl.ds(pl.multiple_of(16 * row, 16), 16), 0:B]
+
+    tops_first.deal.start()
     spread_e.gather()
+    tops_first.gather()
     spread_p.forward()
     spread_p.wait()
-    panel(0, spread_e)
-    panel(1, Spread(2, er.at[1], ec.at[1]))
+    panel(0, spread_e, tops_first)
+    panel(1, Spread(2, er.at[1], ec.at[1]), Tops(2, top1.at[1]))
 
     def last(n):
         lanes = pl.ds(pl.multiple_of(n * B, B), B)
@@ -557,16 +602,17 @@
             vmem(2, 1024, B), vmem(2, B, 1024),
             vmem(2, 1024, B), vmem(2, B, 1024),
             vmem(B, 1024),
+            vmem(2, 16, 80, B), vmem(2, B, 1024),
+            vmem(2, 8, 80, B), vmem(2, 8, 80, B), vmem(2, 16, 16, 1024),
             vmem(2, 1024, B), vmem(2, B, 1024),
-            vmem(2, 512, B), vmem(2, 8, 64, B), vmem(2, 16, 16, 1024),
-            vmem(2, 1024, B), vmem(2, B, 1024),
-            vmem(2, 2, 16, 16, B), vmem(2, 16, 32, B), vmem(2, 16, 48, B),
+            vmem(2, 2, 16, 16, B), vmem(2, 16, 16, B), vmem(2, 16, 16, B),
+            vmem(2, 16, 16, B), vmem(2, 16, 32, B),
             vmem(B, 2 * B),
             vmem(1024, 2 * B), vmem(2 * B, 1024),
-            vmem(2, B, B),
+            vmem(5, B, B),
             pltpu.SemaphoreType.DMA((4,)),
-            pltpu.SemaphoreType.DMA((480,)),
-            pltpu.SemaphoreType.DMA((480,)),
+            pltpu.SemaphoreType.DMA((544,)),
+            pltpu.SemaphoreType.DMA((544,)),
         ],
         compiler_params=pltpu.CompilerParams(
             collective_id=0, has_side_effects=True, vmem_limit_bytes=60 * 1024 * 1024

time: 255 us -> 231 us (0.906)
  Pallas kernels: 248 us -> 225 us
    pallas_call x1, Pallas kernels: 248 us -> 225 us  [shards(): pl.pallas_call(kernel, out_shape=(jax.ShapeDtypeStruct((1024, 1024), F32)...]
where the time goes in v2:
time: 231 us
  Pallas kernels  225 us (97%)
  local copies, waits for them, and re-layouts  5.64 us (2%)
    pallas_call x1, Pallas kernels, shards(): pl.pallas_call(kernel, out_shape=(jax.ShapeDtypeStruct((1024, 1024), F32)...  225 us
    unnamed x4, local copies, waits for them, and re-layouts  5.64 us

profile of v2, /device:TPU:1, one launch (start us, length us, event | category | flops | bytes accessed | tf_op | source)
XLA Modules:
  0.0 231.3 jit_solution(17947950560741472425)
XLA Ops:
  0.6 225.0 %shard_map.30 = (f32[1024,1024]{1,0:T(8,128)}, f32[2,256,256]{2,1,0:T(8,128)}) custom-call(f32[1024,1024]{1,0:T(8,128)} %a_ref.1), custom_call_target="tpu_custom_call" | custom-call | tf_op jit(solution)/shard_map/pallas_call | solution.py:591
  225.7 0.0 copy-start
  225.7 4.8 %copy.5 = f32[1024,1024]{1,0:T(8,128)} copy(f32[1024,1024]{1,0:T(8,128)} %get-tuple-element.4) | data formatting | bytes 8388608
  230.5 0.0 copy-done
  230.5 0.8 copy.6
Async XLA Ops:
  225.7 4.9 %copy-start = (f32[2,256,256]{2,1,0:T(8,128)S(1)}, f32[2,256,256]{2,1,0:T(8,128)}, u32[]{:S(2)}) copy-start(f32[2,256,256]{2,1,0:T(8,128)} %get-tuple-element.5) | copy-start | bytes 1572868

commit v3 on v2

--- a/solution.py
+++ b/solution.py
@@ -92,6 +92,7 @@
     def finish(self):
         for wait in self.sent:
             wait()
+        self.sent = []
 
 
 class Exchange:
@@ -386,9 +387,7 @@
         cross.start()
         loop(2, 4, product_cols)
         ring.start()
-        if p == 0:
-            spread_e.forward()
-        else:
+        if p == 1:
             tops1.gather()
             spread_e.gather()
 
@@ -427,6 +426,8 @@
         inner_reduce()
         tops2.gather()
         cholesky_block(aug, 2)
+        if p == 0:
+            spread_e.forward()
         cholesky_block(aug, 3)
 
         upper = jnp.where(
@@ -559,8 +560,14 @@
     tops_first.gather()
     spread_p.forward()
     spread_p.wait()
+    first = comm.used
     panel(0, spread_e, tops_first)
-    panel(1, Spread(2, er.at[1], ec.at[1]), Tops(2, top1.at[1]))
+    comm.finish()
+    comm.used = 0
+    spread_next = Spread(2, er.at[1], ec.at[1])
+    tops_next = Tops(2, top1.at[1])
+    comm.used = first
+    panel(1, spread_next, tops_next)
 
     def last(n):
         lanes = pl.ds(pl.multiple_of(n * B, B), B)
@@ -611,8 +618,8 @@
             vmem(1024, 2 * B), vmem(2 * B, 1024),
             vmem(5, B, B),
             pltpu.SemaphoreType.DMA((4,)),
-            pltpu.SemaphoreType.DMA((544,)),
-            pltpu.SemaphoreType.DMA((544,)),
+            pltpu.SemaphoreType.DMA((304,)),
+            pltpu.SemaphoreType.DMA((304,)),
         ],
         compiler_params=pltpu.CompilerParams(
             collective_id=0, has_side_effects=True, vmem_limit_bytes=60 * 1024 * 1024

time: 231 us -> 227 us (0.983)
  Pallas kernels: 225 us -> 221 us
    pallas_call x1, Pallas kernels: 225 us -> 221 us  [shards(): pl.pallas_call(kernel, out_shape=(jax.ShapeDtypeStruct((1024, 1024), F32)...]
where the time goes in v3:
time: 227 us
  Pallas kernels  221 us (97%)
  local copies, waits for them, and re-layouts  5.64 us (2%)
    pallas_call x1, Pallas kernels, shards(): pl.pallas_call(kernel, out_shape=(jax.ShapeDtypeStruct((1024, 1024), F32)...  221 us
    unnamed x4, local copies, waits for them, and re-layouts  5.64 us

profile of v3, /device:TPU:1, one launch (start us, length us, event | category | flops | bytes accessed | tf_op | source)
XLA Modules:
  0.0 226.8 jit_solution(674628458528116684)
XLA Ops:
  0.6 220.5 %shard_map.30 = (f32[1024,1024]{1,0:T(8,128)}, f32[2,256,256]{2,1,0:T(8,128)}) custom-call(f32[1024,1024]{1,0:T(8,128)} %a_ref.1), custom_call_target="tpu_custom_call" | custom-call | tf_op jit(solution)/shard_map/pallas_call | solution.py:598
  221.2 0.0 copy-start
  221.2 4.8 %copy.5 = f32[1024,1024]{1,0:T(8,128)} copy(f32[1024,1024]{1,0:T(8,128)} %get-tuple-element.4) | data formatting | bytes 8388608
  226.0 0.0 copy-done
  226.0 0.8 copy.6
Async XLA Ops:
  221.2 4.9 %copy-start = (f32[2,256,256]{2,1,0:T(8,128)S(1)}, f32[2,256,256]{2,1,0:T(8,128)}, u32[]{:S(2)}) copy-start(f32[2,256,256]{2,1,0:T(8,128)} %get-tuple-element.5) | copy-start | bytes 1572868

commit v4 on v3

--- a/solution.py
+++ b/solution.py
@@ -548,7 +548,6 @@
     spread_e = Spread(1, er.at[0], ec.at[0])
     tops_first = Tops(1, top1.at[0])
     spread_p.deal(True)
-    spread_e.deal(False)
     spread_p.gather()
 
     @pl.when(col == 1)
@@ -556,9 +555,10 @@
         top1[0, row] = pc[0, pl.ds(pl.multiple_of(16 * row, 16), 16), 0:B]
 
     tops_first.deal.start()
-    spread_e.gather()
+    spread_e.deal(False)
     tops_first.gather()
     spread_p.forward()
+    spread_e.gather()
     spread_p.wait()
     first = comm.used
     panel(0, spread_e, tops_first)

time: 227 us -> 232 us (1.022); the launches traced: 227 us -> 229 us
    pallas_call x1, Pallas kernels: 221 us -> 223 us  [shards(): pl.pallas_call(kernel, out_shape=(jax.ShapeDtypeStruct((1024, 1024), F32)...]
where the time goes in v4:
time: 232 us; the launch traced here: 229 us
  Pallas kernels  223 us (96%)
  local copies, waits for them, and re-layouts  5.64 us (2%)
    pallas_call x1, Pallas kernels, shards(): pl.pallas_call(kernel, out_shape=(jax.ShapeDtypeStruct((1024, 1024), F32)...  223 us
    unnamed x4, local copies, waits for them, and re-layouts  5.64 us

profile of v4, /device:TPU:1, one launch (start us, length us, event | category | flops | bytes accessed | tf_op | source)
XLA Modules:
  0.0 229.4 jit_solution(595101884579980119)
XLA Ops:
  0.6 223.2 %shard_map.30 = (f32[1024,1024]{1,0:T(8,128)}, f32[2,256,256]{2,1,0:T(8,128)}) custom-call(f32[1024,1024]{1,0:T(8,128)} %a_ref.1), custom_call_target="tpu_custom_call" | custom-call | tf_op jit(solution)/shard_map/pallas_call | solution.py:598
  223.8 0.0 copy-start
  223.8 4.8 %copy.5 = f32[1024,1024]{1,0:T(8,128)} copy(f32[1024,1024]{1,0:T(8,128)} %get-tuple-element.4) | data formatting | bytes 8388608
  228.7 0.0 copy-done
  228.7 0.8 copy.6
Async XLA Ops:
  223.8 4.9 %copy-start = (f32[2,256,256]{2,1,0:T(8,128)S(1)}, f32[2,256,256]{2,1,0:T(8,128)}, u32[]{:S(2)}) copy-start(f32[2,256,256]{2,1,0:T(8,128)} %get-tuple-element.5) | copy-start | bytes 1572868
